TPU v7x, 32 devices: a whole 2x2x4 slice. The times are simulated.
32 devices in a mesh: member: 4 (over x, core), tile: 8 (over z, y).
Axes of the slice: x: 2, y: 2, z: 4, core: 2. Of those that a mesh axis runs over, the one named last changes fastest.
Arguments:
- noisy_state: float32 [4, 4, 512, 128], P('member', None, 'tile'), may hold values from -8 to 8
- churn_noise: float32 [4, 4, 512, 128], P('member', None, 'tile'), may hold values from -6 to 6
- coarse_cond: bfloat16 [16, 512, 128], P('member', 'tile'), may hold values from -6 to 6
- land_mask: int32 [512, 128], P('tile'), may hold values 0 or 1
- step_index: int32 [1], replicated, may hold values from 9 to 16
- owners: int32 [8, 16, 1], replicated, may hold values from 0 to 7; in each aligned block of 16 rows (0 to 15, 16 to 31, ..., all dimensions but the last counted through in order) at most 2 rows name the same one
- patch_rows: int32 [8, 16], replicated, may hold values from 0 to 32
- patch_cols: int32 [8, 16], replicated, may hold values from 0 to 96
- w_in: bfloat16 [128, 20], replicated, may hold values from -1.25 to 1.25
- b_in: float32 [128], replicated, may hold values from -3 to 3
- w_emb: float32 [128, 128], replicated, may hold values from -0.5 to 0.5
- w_conv: bfloat16 [9, 128, 128], replicated, may hold values from -0.1875 to 0.1875
- gn_gain: float32 [128], replicated, may hold values from 0.5 to 1.5
- gn_bias: float32 [128], replicated, may hold values from -3 to 3
- w_out: bfloat16 [4, 128], replicated, may hold values from -0.5 to 0.5
- b_out: float32 [4], replicated, may hold values from -3 to 3
Outputs:
- next_state: float32 [4, 4, 512, 128], P('member', None, 'tile')
Inputs may be any that keep to these rules, and one draw needn't show every extreme that they name: `owners`: at most 2 patches of one worker's list lie on one owner tile, and some worker has exactly 2 on one; every tile owns a patch of some list.
All inputs are finite; a program needn't handle non-finite values. No bound on the sum of `land_mask` on one device may be relied on, other than what follows from the above.
Results may differ from a plain program's by a relative error of at most 0.00041.
Values may be sent and summed in bfloat16 or wider, within the bound.
A program may use at most 64 MiB of HBM per device.

v0:
```python
import jax
import jax.numpy as jnp
from jax import lax
from jax.sharding import PartitionSpec as P

PH = 32
PW = 32
NSTEPS = 18


SIGMA_DATA = 0.5
GAMMA = 0.25


def sigma_at(index_value):
    top_root = 800.0 ** (1.0 / 7.0)
    low_root = 0.002 ** (1.0 / 7.0)
    fraction = index_value.astype(jnp.float32) / (NSTEPS - 1)
    return (top_root + fraction * (low_root - top_root)) ** 7


def precondition(step_index, w_emb):
    sigma_now = sigma_at(step_index[0])
    sigma_next = sigma_at(step_index[0] + 1)
    sigma_hat = (1.0 + GAMMA) * sigma_now
    sigma_sq_sum = sigma_hat * sigma_hat + SIGMA_DATA * SIGMA_DATA
    scale_in = 1.0 / jnp.sqrt(sigma_sq_sum)
    scale_skip = SIGMA_DATA * SIGMA_DATA / sigma_sq_sum
    scale_out = SIGMA_DATA * sigma_hat / jnp.sqrt(sigma_sq_sum)
    churn_scale = jnp.sqrt(GAMMA * (2.0 + GAMMA)) * sigma_now
    noise_level = jnp.log(sigma_hat) / 4.0
    half_width = w_emb.shape[1] // 2
    frequency = jnp.exp(-jnp.log(10000.0) * jnp.arange(half_width, dtype=jnp.float32) / half_width)
    angles = 1000.0 * noise_level * frequency
    features = jnp.concatenate([jnp.cos(angles), jnp.sin(angles)])
    embedding = jnp.dot(w_emb, features, precision=lax.Precision.HIGHEST)
    return (sigma_hat, sigma_next, scale_in, scale_skip, scale_out, churn_scale, embedding)


def window_weights(length):
    position = jnp.arange(length, dtype=jnp.float32)
    return 0.3 + 0.7 * jnp.sin(jnp.pi * (position + 0.5) / length)


def blend_table():
    return (window_weights(PH)[:, None] * window_weights(PW)[None, :]).reshape(-1)


def denoiser(patch_data, net_params, embedding):
    w_in, b_in, w_conv, gn_gain, gn_bias, w_out, b_out = net_params
    pre_act = (
        jnp.dot(w_in, patch_data, preferred_element_type=jnp.float32) + (b_in + embedding)[:, None]
    )
    hidden = jax.nn.silu(pre_act).astype(jnp.bfloat16)
    cell_count = hidden.shape[1]
    padded = jnp.pad(hidden, ((0, 0), (PW + 1, PW + 1)))
    column = jnp.arange(cell_count) % PW
    left_ok = (column >= 1).astype(jnp.bfloat16)
    right_ok = (column <= PW - 2).astype(jnp.bfloat16)
    convolved = jnp.zeros((w_conv.shape[1], cell_count), jnp.float32)
    for row_step in (-1, 0, 1):
        for col_step in (-1, 0, 1):
            start_cell = PW + 1 + row_step * PW + col_step
            shifted = lax.slice_in_dim(padded, start_cell, start_cell + cell_count, axis=1)
            if col_step == -1:
                shifted = shifted * left_ok[None, :]
            if col_step == 1:
                shifted = shifted * right_ok[None, :]
            tap_index = (row_step + 1) * 3 + (col_step + 1)
            convolved = convolved + jnp.dot(
                w_conv[tap_index], shifted, preferred_element_type=jnp.float32
            )
    grouped = convolved.reshape(32, -1)
    group_mean = jnp.mean(grouped, axis=1, keepdims=True)
    group_var = jnp.mean((grouped - group_mean) ** 2, axis=1, keepdims=True)
    normed = ((grouped - group_mean) * lax.rsqrt(group_var + 1e-06)).reshape(convolved.shape)
    normed = normed * gn_gain[:, None] + gn_bias[:, None]
    residual = (hidden.astype(jnp.float32) + jax.nn.silu(normed)).astype(jnp.bfloat16)
    return jnp.dot(w_out, residual, preferred_element_type=jnp.float32) + b_out[:, None]


def extract_patches(inputs, row_list, col_list):
    channels = inputs.shape[0]
    zero_index = jnp.zeros((), jnp.int32)

    def one_patch(row_start, col_start):
        sliced = lax.dynamic_slice(inputs, (zero_index, row_start, col_start), (channels, PH, PW))
        return sliced.reshape(channels, PH * PW)

    return jax.vmap(one_patch)(row_list, col_list)


def place_patches(running_total, blended, row_list, col_list):
    variables = blended.shape[1]
    zero_index = jnp.zeros((), jnp.int32)

    def add_one(slot_index, running):
        corner = (zero_index, row_list[slot_index], col_list[slot_index])
        current = lax.dynamic_slice(running, corner, (variables, PH, PW))
        return lax.dynamic_update_slice(
            running, current + blended[slot_index].reshape(variables, PH, PW), corner
        )

    return lax.fori_loop(0, blended.shape[0], add_one, running_total)


def coverage(row_list, col_list, live_mask, row_count, col_count):
    row_offset = (jnp.arange(row_count)[None, :] - row_list[:, None]).astype(jnp.float32)
    col_offset = (jnp.arange(col_count)[None, :] - col_list[:, None]).astype(jnp.float32)
    row_weight = (0.3 + 0.7 * jnp.sin(jnp.pi * (row_offset + 0.5) / PH)) * (
        (row_offset >= 0) & (row_offset < PH)
    ).astype(jnp.float32)
    col_weight = (0.3 + 0.7 * jnp.sin(jnp.pi * (col_offset + 0.5) / PW)) * (
        (col_offset >= 0) & (col_offset < PW)
    ).astype(jnp.float32)
    row_weight = row_weight * live_mask[:, None]
    return jnp.dot(row_weight.T, col_weight, precision=lax.Precision.HIGHEST)


def finish_step(x_hat, accumulated, weights, land_mask, constants):
    sigma_hat, sigma_next, scale_in, scale_skip, scale_out, churn_scale, embedding = constants
    land_value = land_mask.astype(jnp.float32)
    denoised = (
        land_value
        * (weights * scale_skip * x_hat + scale_out * accumulated)
        / jnp.maximum(weights, 0.25)
    )
    return x_hat + (sigma_next - sigma_hat) / sigma_hat * (x_hat - denoised)


def body(
    noisy_state,
    churn_noise,
    coarse_cond,
    land_mask,
    step_index,
    owners,
    patch_rows,
    patch_cols,
    w_in,
    b_in,
    w_emb,
    w_conv,
    gn_gain,
    gn_bias,
    w_out,
    b_out,
):
    self_tile = lax.axis_index("tile")
    tile_count = lax.axis_size("tile")
    tile_rows = noisy_state.shape[2]
    tile_cols = noisy_state.shape[3]
    variables = noisy_state.shape[1]
    constants = precondition(step_index, w_emb)
    scale_in = constants[2]
    churn_scale = constants[5]
    embedding = constants[6]
    net_params = (w_in, b_in, w_conv, gn_gain, gn_bias, w_out, b_out)
    blend = blend_table()
    x_hat = noisy_state[0] + churn_scale * churn_noise[0]
    scaled = (scale_in * x_hat).astype(jnp.bfloat16)
    cond_part = lax.all_gather(coarse_cond, "member", axis=0, tiled=True)
    local_in = jnp.concatenate([cond_part, scaled], axis=0)
    owner_table = owners[:, :, 0]
    my_owner = owner_table[self_tile]
    my_rows = patch_rows[self_tile]
    my_cols = patch_cols[self_tile]
    everything = lax.all_gather(local_in, "tile", axis=1, tiled=True)
    row_global = my_owner * tile_rows + my_rows
    my_patches = extract_patches(everything, row_global, my_cols)
    blended = (
        lax.map(lambda patch_data: denoiser(patch_data, net_params, embedding), my_patches)
        * blend[None, None, :]
    )
    partial_value = place_patches(
        jnp.zeros((variables, tile_rows * tile_count, tile_cols), jnp.float32),
        blended,
        row_global,
        my_cols,
    )
    accumulated = lax.psum_scatter(partial_value, "tile", scatter_dimension=1, tiled=True)
    live_mask = (owners.reshape(-1) == self_tile).astype(jnp.float32)
    weights = coverage(
        patch_rows.reshape(-1), patch_cols.reshape(-1), live_mask, tile_rows, tile_cols
    )
    return finish_step(x_hat, accumulated, weights, land_mask, constants)[None]


def solution(mesh):
    return jax.shard_map(
        body,
        mesh=mesh,
        in_specs=(
            P("member", None, "tile", None),
            P("member", None, "tile", None),
            P("member", "tile", None),
            P("tile", None),
            P(),
            P(),
            P(),
            P(),
            P(),
            P(),
            P(),
            P(),
            P(),
            P(),
            P(),
            P(),
        ),
        out_specs=P("member", None, "tile", None),
        check_vma=False,
    )
```

profile of v0, /device:TPU:1, one launch (start us, length us, event | category | flops | bytes accessed | tf_op | source)
XLA Modules:
  0.0 391.0 jit_solution(10954234211027769788)
XLA Ops:
  7.3 7.3 %all_gather.6 = bf16[16,64,128]{2,1,0:T(8,128)(2,1)S(1)} all-gather(bf16[4,64,128]{2,1,0:T(8,128)(2,1)} %param.22), channel_id=1, replica_groups=mesh['member'=4,'tile'=8] {'member'}, dimensions={0}, use_global_device_ids=true | all-gather | bytes 327680 | tf_op jit(solution)/shard_map/all_gather | solution.py:162
  19.9 50.9 %all-gather.2.cloned.1.call-done = bf16[20,512,128]{2,1,0:T(8,128)(2,1)} async-done(((bf16[20,64,128]{2,1,0:T(8,128)(2,1)}), bf16[20,512,128]{2,1,0:T(8,128)(2,1)}) %all-gather.2.cloned.1.call-update) | async-done | bytes 2621456 | tf_op jit(solution)/shard_map/all_gather | solution.py:168
  70.8 47.0 %while.28 = (s32[]{:T(128)}, bf16[20,512,128]{2,1,0:T(8,128)(2,1)}, s32[16,3]{0,1:T(4,128)S(1)}, bf16[16,20,32,32]{3,2,1,0:T(8,128)(2,1)S(1)}, s32[]{:T(128)}) while((s32[]{:T(128)}, bf16[20,512,128]{2,1,0:T(8,128)(2,1)}, s32[16,3]{0,1:T(4,128)S(1)}, bf16[16,20,32,32]{3,2,1,0:T(8,128)(2,1)S(1)}, s32[]{:T(128)}) %tuple.71), condition=%wide.while_cond, body=%wide.while_body.sunk | while | flops 2 | bytes 204917 | solution.py:87
  71.4 2.3 bitcast_dynamic-update-slice_fusion.2
  74.3 2.3 bitcast_dynamic-update-slice_fusion.2
  77.3 2.3 bitcast_dynamic-update-slice_fusion.2
  80.2 2.3 bitcast_dynamic-update-slice_fusion.2
  83.2 2.3 bitcast_dynamic-update-slice_fusion.2
  86.1 2.3 bitcast_dynamic-update-slice_fusion.2
  89.0 2.3 bitcast_dynamic-update-slice_fusion.2
  92.0 2.3 bitcast_dynamic-update-slice_fusion.2
  94.9 2.3 bitcast_dynamic-update-slice_fusion.2
  97.9 2.3 bitcast_dynamic-update-slice_fusion.2
  100.8 2.3 bitcast_dynamic-update-slice_fusion.2
  103.8 2.3 bitcast_dynamic-update-slice_fusion.2
  106.7 2.3 bitcast_dynamic-update-slice_fusion.2
  109.6 2.3 bitcast_dynamic-update-slice_fusion.2
  112.6 2.3 bitcast_dynamic-update-slice_fusion.2
  115.5 2.3 bitcast_dynamic-update-slice_fusion.2
  117.8 3.6 reshape.213
  121.5 83.5 %while.26 = (s32[]{:T(128)}, f32[16,4,1024]{2,1,0:T(4,128)S(1)}, bf16[16,20,1024]{2,1,0:T(8,128)(2,1)}, bf16[128,20]{0,1:T(8,128)(2,1)S(1)}, f32[128,1]{0,1:T(1,...) while((s32[]{:T(128)}, f32[16,4,1024]{2,1,0:T(4,128)S(1)}, ...), condition=%wide.region_5.6_spmd, body=%wide.region_0.5_spmd.sunk | while | flops 315248672 | bytes 13240449 | solution.py:172
  205.1 112.9 %while.27 = (s32[]{:T(128)}, f32[4,512,128]{2,1,0:T(8,128)S(1)}, s32[16]{0:T(128)S(1)}, s32[16]{0:T(128)S(1)}, f32[16,4,1024]{2,1,0:T(4,128)S(1)}, /*index=5*/s32[]{:T(128)}, s32[]{:T(128)}, s32[]{:T(128)}, s32[]{:T(128)}) while((s32[]{:T(128)}, f32[4,512,128]{2,1,0:T(8,128)S(1)}, s32[16]{0:T(128)S(1)}, s32[16]{0:T(128)S(1)}, ...), condition=%wide.region_7.8_spmd, body=%wide.region_6.7_spmd.sunk | while | flops 4104 | bytes 147657 | solution.py:104
  210.4 1.9 dynamic_update_slice.18
  217.5 1.9 dynamic_update_slice.18
  224.6 1.9 dynamic_update_slice.18
  231.8 1.9 dynamic_update_slice.18
  238.9 1.9 dynamic_update_slice.18
  246.0 1.9 dynamic_update_slice.18
  260.3 1.9 dynamic_update_slice.18
  267.4 1.9 dynamic_update_slice.18
  281.7 1.9 dynamic_update_slice.18
  320.3 62.2 %reduce-scatter.2.cloned.1.call-done = f32[4,64,128]{2,1,0:T(8,128)} async-done(((f32[4,512,128]{2,1,0:T(8,128)}), f32[4,64,128]{2,1,0:T(8,128)}) %reduce-scatter.2.cloned.1.call-update) | async-done | bytes 131088 | tf_op jit(solution)/shard_map/reduce_scatter | solution.py:181
  (558 shorter events, 135.2 us)
Async XLA Ops:
  6.5 12.4 %copy-start = (f32[128,128]{1,0:T(8,128)S(1)}, f32[128,128]{1,0:T(8,128)}, u32[]{:S(2)}) copy-start(f32[128,128]{1,0:T(8,128)} %param.30) | copy-start | bytes 196612
  6.5 64.2 %all-gather.2.cloned.1.call-start = ((), (), s32[]{:S(2)}) async-start(), calls=%async_computation.1 | async-start | bytes 2949120 | tf_op jit(solution)/shard_map/all_gather | solution.py:168
  16.4 366.1 %reduce-scatter.2.cloned.1.call-start = ((), (), s32[]{:S(2)}) async-start(), calls=%async_computation.2 | async-start | bytes 1179648 | tf_op jit(solution)/shard_map/reduce_scatter | solution.py:181
  19.8 101.6 %copy-start.1 = (bf16[9,128,128]{2,1,0:T(8,128)(2,1)S(1)}, bf16[9,128,128]{2,1,0:T(8,128)(2,1)}, u32[]{:S(2)}) copy-start(bf16[9,128,128]{2,1,0:T(8,128)(2,1)} %param.31) | copy-start | bytes 884740
  19.8 101.6 %copy-start.9 = (bf16[128,20]{0,1:T(8,128)(2,1)S(1)}, bf16[128,20]{0,1:T(8,128)(2,1)}, u32[]{:S(2)}) copy-start(bf16[128,20]{0,1:T(8,128)(2,1)} %param.28) | copy-start | bytes 15364
  19.8 101.6 %copy-start.10 = (bf16[4,128]{1,0:T(4,128)(2,1)S(1)}, bf16[4,128]{1,0:T(4,128)(2,1)}, u32[]{:S(2)}) copy-start(bf16[4,128]{1,0:T(4,128)(2,1)} %param.34) | copy-start | bytes 3076
  19.9 101.6 %copy-start.11 = (f32[128]{0:T(128)S(1)}, f32[128]{0:T(128)}, u32[]{:S(2)}) copy-start(f32[128]{0:T(128)} %param.32) | copy-start | bytes 1540
  19.9 101.6 %copy-start.12 = (f32[128]{0:T(128)S(1)}, f32[128]{0:T(128)}, u32[]{:S(2)}) copy-start(f32[128]{0:T(128)} %param.33) | copy-start | bytes 1540
  19.9 101.6 %copy-start.13 = (f32[4]{0:T(128)S(1)}, f32[4]{0:T(128)}, u32[]{:S(2)}) copy-start(f32[4]{0:T(128)} %param.35) | copy-start | bytes 52
  204.9 114.2 %copy-start.6 = (s32[8,16]{1,0:T(8,128)S(1)}, s32[8,16]{1,0:T(8,128)}, u32[]{:S(2)}) copy-start(s32[8,16]{1,0:T(8,128)} %param.26) | copy-start | bytes 1540
  204.9 114.3 %copy-start.8 = (s32[8,16]{1,0:T(8,128)S(1)}, s32[8,16]{1,0:T(8,128)}, u32[]{:S(2)}) copy-start(s32[8,16]{1,0:T(8,128)} %param.27) | copy-start | bytes 1540
  204.9 114.4 %copy-start.7 = (s32[8,16,1]{1,2,0:T(1,128)S(1)}, s32[8,16,1]{1,2,0:T(1,128)}, u32[]{:S(2)}) copy-start(s32[8,16,1]{1,2,0:T(1,128)} %param.25) | copy-start | bytes 1540
  205.0 114.5 %copy-start.5 = (s32[64,128]{1,0:T(8,128)S(1)}, s32[64,128]{1,0:T(8,128)}, u32[]{:S(2)}) copy-start(s32[64,128]{1,0:T(8,128)} %param.23) | copy-start | bytes 98308
  205.0 177.5 %copy-start.3 = (f32[1,4,64,128]{3,2,1,0:T(8,128)S(1)}, f32[1,4,64,128]{3,2,1,0:T(8,128)}, u32[]{:S(2)}) copy-start(f32[1,4,64,128]{3,2,1,0:T(8,128)} %param.20) | copy-start | bytes 393220
  205.0 177.5 %copy-start.4 = (f32[1,4,64,128]{3,2,1,0:T(8,128)S(1)}, f32[1,4,64,128]{3,2,1,0:T(8,128)}, u32[]{:S(2)}) copy-start(f32[1,4,64,128]{3,2,1,0:T(8,128)} %param.21) | copy-start | bytes 393220
  318.1 1.0 copy-start.2
Sparse Core Ops, SparseCore 0:
  16.5 54.1 all-gather.1
  319.2 63.3 reduce-scatter.1
where the time goes:
time: 396 us; the launch traced here: 391 us
  waiting for transfers between devices  113 us (29%)
  local copies, waits for them, and re-layouts  112 us (28%)
  matrix products  67.8 us (17%)
  loops' own time  63.6 us (16%)
  between operations  14.6 us (4%)
  other arithmetic  12.9 us (3%)
  blocking collectives  7.3 us (2%)
    reduce_scatter x1, waiting for transfers between devices, body(): lax.psum_scatter(partial_value, 'tile', scatter_dimension=1, tiled=True)  62.2 us
    another operation x1, loops' own time, place_patches(): return lax.fori_loop(0, blended.shape[0], add_one, running_total)  61.6 us
    all_gather x1, waiting for transfers between devices, body(): everything = lax.all_gather(local_in, 'tile', axis=1, tiled=True)  50.9 us
    gather x48, local copies, waits for them, and re-layouts  46.8 us
    dot_general x144, matrix products, denoiser(): jnp.dot(w_conv[tap_index], shifted, preferred_element_type=jnp.float32)  42.4 us
    dynamic_update_slice x16, local copies, waits for them, and re-layouts, add_one(): lax.dynamic_update_slice(running, current + blended[slot_index].reshape(v...  28.7 us
    dynamic_slice x32, local copies, waits for them, and re-layouts, add_one(): corner = (zero_index, row_list[slot_index], col_list[slot_index])  19.6 us
    dot_general x16, matrix products, denoiser(): jnp.dot(w_in, patch_data, preferred_element_type=jnp.float32)  18.3 us
  transfers between devices with their start and end apart: 2, of which 2 were waited for; matrix products, arithmetic and copies ran while one was open for 1% of the time, Pallas kernels for 0%

commit v1 on v0

v1 whole, which is shorter than its diff:
```python
import functools

import jax
import jax.numpy as jnp
import numpy as np
from jax import lax
from jax.experimental import pallas as pl
from jax.experimental.pallas import tpu as pltpu
from jax.sharding import PartitionSpec as P

PH = 32
PW = 32
NSTEPS = 18


SIGMA_DATA = 0.5
GAMMA = 0.25


def sigma_at(index_value):
    top_root = 800.0 ** (1.0 / 7.0)
    low_root = 0.002 ** (1.0 / 7.0)
    fraction = index_value.astype(jnp.float32) / (NSTEPS - 1)
    return (top_root + fraction * (low_root - top_root)) ** 7


def precondition(step_index, w_emb):
    sigma_now = sigma_at(step_index[0])
    sigma_next = sigma_at(step_index[0] + 1)
    sigma_hat = (1.0 + GAMMA) * sigma_now
    sigma_sq_sum = sigma_hat * sigma_hat + SIGMA_DATA * SIGMA_DATA
    scale_in = 1.0 / jnp.sqrt(sigma_sq_sum)
    scale_skip = SIGMA_DATA * SIGMA_DATA / sigma_sq_sum
    scale_out = SIGMA_DATA * sigma_hat / jnp.sqrt(sigma_sq_sum)
    churn_scale = jnp.sqrt(GAMMA * (2.0 + GAMMA)) * sigma_now
    noise_level = jnp.log(sigma_hat) / 4.0
    half_width = w_emb.shape[1] // 2
    frequency = jnp.exp(-jnp.log(10000.0) * jnp.arange(half_width, dtype=jnp.float32) / half_width)
    angles = 1000.0 * noise_level * frequency
    features = jnp.concatenate([jnp.cos(angles), jnp.sin(angles)])
    embedding = jnp.dot(w_emb, features, precision=lax.Precision.HIGHEST)
    return (sigma_hat, sigma_next, scale_in, scale_skip, scale_out, churn_scale, embedding)


def window_weights(length):
    position = np.arange(length, dtype=np.float64)
    return 0.3 + 0.7 * np.sin(np.pi * (position + 0.5) / length)


def gather_kernel(axis_size, part_ref, whole_ref, send_sem, recv_sem, local_sem):
    me = lax.axis_index("member")
    depth = part_ref.shape[0]
    barrier = pltpu.get_barrier_semaphore()
    for step in range(1, axis_size):
        pl.semaphore_signal(
            barrier,
            inc=1,
            device_id={"member": lax.rem(me + step, axis_size)},
            device_id_type=pl.DeviceIdType.MESH,
        )
    pl.semaphore_wait(barrier, axis_size - 1)
    own = whole_ref.at[pl.ds(me * depth, depth)]
    copies = []
    for step in range(1, axis_size):
        copy = pltpu.make_async_remote_copy(
            src_ref=part_ref,
            dst_ref=own,
            send_sem=send_sem.at[step - 1],
            recv_sem=recv_sem.at[step - 1],
            device_id={"member": lax.rem(me + step, axis_size)},
            device_id_type=pl.DeviceIdType.MESH,
        )
        copy.start()
        copies.append(copy)
    local = pltpu.make_async_copy(part_ref, own, local_sem)
    local.start()
    local.wait()
    for copy in copies:
        copy.wait()


def gather_members(part, axis_size):
    shape = (part.shape[0] * axis_size,) + part.shape[1:]
    return pl.pallas_call(
        functools.partial(gather_kernel, axis_size),
        out_shape=jax.ShapeDtypeStruct(shape, part.dtype),
        in_specs=[pl.BlockSpec(memory_space=pltpu.VMEM)],
        out_specs=pl.BlockSpec(memory_space=pltpu.VMEM),
        scratch_shapes=[
            pltpu.SemaphoreType.DMA((axis_size - 1,)),
            pltpu.SemaphoreType.DMA((axis_size - 1,)),
            pltpu.SemaphoreType.DMA,
        ],
        compiler_params=pltpu.CompilerParams(collective_id=0, has_side_effects=True),
    )(part)


LEAD = 8
K_IN = 32


def silu(value):
    half = 0.5 * value
    return half + half * jnp.tanh(half)


def group_sum(value):
    lane = lax.broadcasted_iota(jnp.int32, value.shape, 1)
    width = value.shape[1]
    pair = value + jnp.where(
        lane % 2 == 0, pltpu.roll(value, width - 1, 1), pltpu.roll(value, 1, 1)
    )
    return pair + jnp.where(
        lane % 4 < 2, pltpu.roll(pair, width - 2, 1), pltpu.roll(pair, 2, 1)
    )


def tile_kernel(
    scalars,
    owners,
    patch_rows,
    patch_cols,
    b_out,
    cond,
    noisy,
    churn,
    land,
    bias_in,
    w_in,
    w_conv,
    gn_gain,
    gn_bias,
    w_out,
    blend_cells,
    blend_lanes,
    out,
    row_list,
    col_list,
    inputs,
    w_square,
    hidden,
    total,
    taps,
    w_pairs,
    conv,
    weights,
    flat,
):
    self_tile = lax.axis_index("tile")
    channels = w_conv.shape[1]
    variables, tile_rows, tile_cols = noisy.shape
    cond_channels = cond.shape[0]
    scale_in = scalars[0]
    churn_scale = scalars[1]
    scale_skip = scalars[2]
    scale_out = scalars[3]
    step_ratio = scalars[4]

    def note_patch(index, count):
        row_list[count] = patch_rows[index]
        col_list[count] = patch_cols[index]
        return count + (owners[index] == self_tile).astype(jnp.int32)

    count = lax.fori_loop(0, owners.shape[0], note_patch, jnp.int32(0), unroll=8)

    for channel in range(cond_channels):
        inputs[channel * tile_rows : (channel + 1) * tile_rows, :] = cond[channel].astype(
            jnp.float32
        )
    for variable in range(variables):
        start = (cond_channels + variable) * tile_rows
        x_hat = noisy[variable] + churn_scale * churn[variable]
        inputs[start : start + tile_rows, :] = (
            (scale_in * x_hat).astype(jnp.bfloat16).astype(jnp.float32)
        )
    used = cond_channels + variables
    inputs[used * tile_rows :, :] = jnp.zeros(
        ((K_IN - used) * tile_rows, tile_cols), jnp.float32
    )
    w_square[...] = jnp.zeros_like(w_square)
    w_square[:, 0:used] = w_in[...].astype(jnp.float32)
    w_first = w_square[...].T[0:K_IN].astype(jnp.bfloat16)
    bias = bias_in[...]

    def hidden_row(row, carry):
        cells = inputs[pl.ds(row, K_IN, stride=tile_rows), :].T.astype(jnp.bfloat16)
        pre_act = jnp.dot(cells, w_first, preferred_element_type=jnp.float32) + bias
        hidden[row, LEAD : LEAD + tile_cols, :] = (
            silu(pre_act).astype(jnp.bfloat16).astype(jnp.float32)
        )
        total[row] = jnp.zeros((tile_cols, channels), jnp.float32)
        return carry

    lax.fori_loop(0, tile_rows, hidden_row, 0, unroll=4)

    zero_block = jnp.zeros((channels, channels), jnp.bfloat16)
    for col in range(3):
        tap = [w_conv[3 * a + col].astype(jnp.float32).T.astype(jnp.bfloat16) for a in range(3)]
        blocks = (
            ((tap[0], zero_block), (tap[1], tap[0])),
            ((tap[2], tap[1]), (zero_block, tap[2])),
        )
        for half in range(2):
            start = (2 * col + half) * 2 * channels
            for k in range(2):
                for o in range(2):
                    w_pairs[
                        start + k * channels : start + (k + 1) * channels,
                        o * channels : (o + 1) * channels,
                    ] = blocks[half][k][o]
        taps[col, 0, :, 0:channels] = jnp.zeros((PW, channels), jnp.bfloat16)
        taps[col, PH // 2, :, channels : 2 * channels] = jnp.zeros((PW, channels), jnp.bfloat16)
    weights[...] = jnp.zeros_like(weights)

    gain = jnp.concatenate([gn_gain[...], gn_gain[...]], axis=1)
    shift = jnp.concatenate([gn_bias[...], gn_bias[...]], axis=1)
    lanes = blend_lanes[...]
    cell_count = PH * PW
    inverse = 1.0 / (4 * cell_count)
    position = lax.broadcasted_iota(jnp.int32, (PW, channels), 0)

    def spread(value):
        value = group_sum(value[:, 0:channels] + value[:, channels : 2 * channels])
        return jnp.concatenate([value, value], axis=1)

    def one_patch(slot, carry):
        row_start = row_list[slot]
        col_start = col_list[slot]
        weights[pl.ds(row_start, PH), :] += pltpu.roll(lanes, col_start, 1)
        for i in range(PH):
            pair = (i + 1) // 2
            lane = 0 if i % 2 else channels
            for col in range(3):
                piece = hidden[row_start + i, pl.ds(col_start + (LEAD - 1 + col), PW), :]
                if col == 0:
                    piece = jnp.where(position == 0, 0.0, piece)
                if col == 2:
                    piece = jnp.where(position == PW - 1, 0.0, piece)
                taps[col, pair, :, lane : lane + channels] = piece.astype(jnp.bfloat16)
        half_cells = cell_count // 2
        left = jnp.concatenate(
            [
                taps[col, half : half + PH // 2].reshape(half_cells, 2 * channels)
                for col in range(3)
                for half in range(2)
            ],
            axis=1,
        )
        convolved = jnp.dot(left, w_pairs[...], preferred_element_type=jnp.float32)
        conv[...] = convolved
        mean = spread(jnp.sum(convolved, axis=0, keepdims=True)) * inverse
        centred = conv[...] - mean
        var = spread(jnp.sum(centred * centred, axis=0, keepdims=True)) * inverse
        scale = lax.rsqrt(var + 1e-06) * gain
        for t in range(PH // 2):
            normed = (conv[t * PW : (t + 1) * PW, :] - mean) * scale + shift
            active = silu(normed)
            for o in range(2):
                i = 2 * t + o
                own = hidden[row_start + i, pl.ds(col_start + LEAD, PW), :]
                residual = (
                    (own + active[:, o * channels : (o + 1) * channels])
                    .astype(jnp.bfloat16)
                    .astype(jnp.float32)
                )
                total[row_start + i, pl.ds(col_start, PW), :] += residual * blend_cells[i]
        return carry

    lax.fori_loop(0, count, one_patch, 0)

    w_square[0:16, :] = jnp.zeros((16, channels), jnp.float32)
    w_square[0:variables, :] = w_out[...].astype(jnp.float32)
    w_last = w_square[0:16, :].astype(jnp.bfloat16)
    w_last = jnp.concatenate([w_last, w_last], axis=1)

    def project(block, carry):
        value = total[pl.ds(block * 8, 8)].reshape(8 * tile_cols, channels)
        high = value.astype(jnp.bfloat16)
        low = (value - high.astype(jnp.float32)).astype(jnp.bfloat16)
        result = lax.dot_general(
            w_last,
            jnp.concatenate([high, low], axis=1),
            (((1,), (1,)), ((), ())),
            preferred_element_type=jnp.float32,
        )
        for j in range(8):
            flat[pl.ds(pl.multiple_of(block * 64, 64) + j * 8, 8), :] = result[
                0:8, j * tile_cols : (j + 1) * tile_cols
            ]
        return carry

    lax.fori_loop(0, tile_rows // 8, project, 0)

    cover = weights[...]
    land_value = land[...].astype(jnp.float32) / jnp.maximum(cover, 0.25)
    for variable in range(variables):
        x_hat = noisy[variable] + churn_scale * churn[variable]
        accumulated = flat[pl.ds(variable, tile_rows, stride=8), :] + b_out[variable] * cover
        denoised = land_value * (cover * scale_skip * x_hat + scale_out * accumulated)
        out[variable] = x_hat + step_ratio * (x_hat - denoised)


def body(
    noisy_state,
    churn_noise,
    coarse_cond,
    land_mask,
    step_index,
    owners,
    patch_rows,
    patch_cols,
    w_in,
    b_in,
    w_emb,
    w_conv,
    gn_gain,
    gn_bias,
    w_out,
    b_out,
):
    sigma_hat, sigma_next, scale_in, scale_skip, scale_out, churn_scale, embedding = precondition(
        step_index, w_emb
    )
    step_ratio = (sigma_next - sigma_hat) / sigma_hat
    zero = jnp.zeros_like(scale_in)
    scalars = jnp.stack(
        [scale_in, churn_scale, scale_skip, scale_out, step_ratio, zero, zero, zero]
    )
    cond = gather_members(coarse_cond, lax.axis_size("member"))
    channels = w_conv.shape[1]
    variables, tile_rows, tile_cols = noisy_state.shape[1:]
    slots = owners.size
    blend = window_weights(PH)[:, None] * window_weights(PW)[None, :]
    blend_cells = jnp.asarray(
        np.broadcast_to(blend[:, :, None], (PH, PW, channels)).astype(np.float32)
    )
    blend_lanes = jnp.asarray(
        np.pad(blend, ((0, 0), (0, tile_cols - PW))).astype(np.float32)
    )
    smem = pl.BlockSpec(memory_space=pltpu.SMEM)
    vmem = pl.BlockSpec(memory_space=pltpu.VMEM)
    f32 = jnp.float32
    result = pl.pallas_call(
        tile_kernel,
        out_shape=jax.ShapeDtypeStruct((variables, tile_rows, tile_cols), f32),
        in_specs=[smem] * 5 + [vmem] * 12,
        out_specs=vmem,
        scratch_shapes=[
            pltpu.SMEM((slots + 1,), jnp.int32),
            pltpu.SMEM((slots + 1,), jnp.int32),
            pltpu.VMEM((K_IN * tile_rows, tile_cols), f32),
            pltpu.VMEM((channels, channels), f32),
            pltpu.VMEM((tile_rows, tile_cols + 2 * LEAD, channels), f32),
            pltpu.VMEM((tile_rows, tile_cols, channels), f32),
            pltpu.VMEM((3, PH // 2 + 1, PW, 2 * channels), jnp.bfloat16),
            pltpu.VMEM((12 * channels, 2 * channels), jnp.bfloat16),
            pltpu.VMEM((PH * PW // 2, 2 * channels), f32),
            pltpu.VMEM((tile_rows, tile_cols), f32),
            pltpu.VMEM((8 * tile_rows, tile_cols), f32),
        ],
        compiler_params=pltpu.CompilerParams(vmem_limit_bytes=40 * 1024 * 1024),
    )(
        scalars,
        owners.reshape(-1),
        patch_rows.reshape(-1),
        patch_cols.reshape(-1),
        b_out,
        cond,
        noisy_state[0],
        churn_noise[0],
        land_mask,
        (b_in + embedding)[None, :],
        w_in,
        w_conv,
        gn_gain[None, :],
        gn_bias[None, :],
        w_out,
        blend_cells,
        blend_lanes,
    )
    return result[None]


def solution(mesh):
    return jax.shard_map(
        body,
        mesh=mesh,
        in_specs=(
            P("member", None, "tile", None),
            P("member", None, "tile", None),
            P("member", "tile", None),
            P("tile", None),
            P(),
            P(),
            P(),
            P(),
            P(),
            P(),
            P(),
            P(),
            P(),
            P(),
            P(),
            P(),
        ),
        out_specs=P("member", None, "tile", None),
        check_vma=False,
    )
```

time: 396 us -> 47.6 us (0.12); the launches traced: 391 us -> 47.1 us
  waiting for transfers between devices: 113 us -> 0 us
  local copies, waits for them, and re-layouts: 112 us -> 7.58 us
  matrix products: 67.8 us -> 0.87 us
  loops' own time: 63.6 us -> 0 us
  Pallas kernels: 0 us -> 36.2 us
  between operations: 14.6 us -> 1.11 us
  other arithmetic: 12.9 us -> 1.4 us
  blocking collectives: 7.3 us -> 0 us
    dot_general x177 -> x0, matrix products: 66.9 us -> none  [the longest x144 42.4 us: denoiser(): jnp.dot(w_conv[tap_index], shifted, preferred_element_type=jnp.float32)]
    another operation x3 -> x0, loops' own time: 63.6 us -> none  [the longest x1 61.6 us: place_patches(): return lax.fori_loop(0, blended.shape[0], add_one, running_total)]
    reduce_scatter x1 -> x0, waiting for transfers between devices: 62.2 us -> none  [body(): lax.psum_scatter(partial_value, 'tile', scatter_dimension=1, tiled=True)]
    all_gather x1 -> x0, waiting for transfers between devices: 50.9 us -> none  [body(): everything = lax.all_gather(local_in, 'tile', axis=1, tiled=True)]
    gather x48 -> x0, local copies, waits for them, and re-layouts: 46.8 us -> none
    pallas_call x0 -> x2, Pallas kernels: none -> 36.2 us  [the longest x1 28.1 us: body(): pl.pallas_call(tile_kernel, out_shape=jax.ShapeDtypeStruct((variables, ti...]
    dynamic_update_slice x16 -> x0, local copies, waits for them, and re-layouts: 28.7 us -> none  [add_one(): lax.dynamic_update_slice(running, current + blended[slot_index].reshape(v...]
    dynamic_slice x48 -> x0, local copies, waits for them, and re-layouts: 19.8 us -> none  [the longest x32 19.6 us: add_one(): corner = (zero_index, row_list[slot_index], col_list[slot_index])]
  transfers between devices with their start and end apart: 2 -> 0, of which waited for: 2 -> 0; matrix products, arithmetic and copies ran while one was open for 1% -> 0% of each run, Pallas kernels for 0% -> 0%
where the time goes in v1:
time: 47.6 us; the launch traced here: 47.1 us
  Pallas kernels  36.2 us (76%)
  local copies, waits for them, and re-layouts  7.58 us (16%)
  other arithmetic  1.4 us (3%)
  between operations  1.11 us (2%)
  matrix products  0.87 us (2%)
    pallas_call x1, Pallas kernels, body(): pl.pallas_call(tile_kernel, out_shape=jax.ShapeDtypeStruct((variables, ti...  28.1 us
    pallas_call x1, Pallas kernels, gather_members(): pl.pallas_call(functools.partial(gather_kernel, axis_size), out_shape=jax...  8.11 us
    unnamed x26, local copies, waits for them, and re-layouts  5.88 us
    unnamed x1, other arithmetic  1.35 us

profile of v1, /device:TPU:1, one launch (start us, length us, event | category | flops | bytes accessed | tf_op | source)
XLA Modules:
  0.0 47.1 jit_solution(15660397420693504798)
XLA Ops:
  0.0 0.0 copy-start
  0.0 0.0 copy-start.2
  1.0 0.8 %reshape.22.patch_rows = s32[128]{0:T(128)S(1)} reshape(s32[8,16]{1,0:T(8,128)} %param.24) | data formatting | bytes 1024 | tf_op jit(solution)/shard_map/reshape | solution.py:365
  1.8 0.8 %reshape.23.patch_cols = s32[128]{0:T(128)S(1)} reshape(s32[8,16]{1,0:T(8,128)} %param.25) | data formatting | bytes 1024 | tf_op jit(solution)/shard_map/reshape | solution.py:366
  2.5 0.1 stack.23.scalars
  2.6 0.1 fusion.4
  2.7 0.0 copy-done
  2.7 0.9 %fusion.1.bias_in = f32[1,128]{1,0:T(1,128)S(1)} fusion(f32[128]{0:T(128)} %param.27, f32[128,128]{1,0:T(8,128)S(1)} %copy-done, f32[64]{0:T(128)S(1)} %get-tuple-element.5, f32[64]{0:T(128)S(1)} %get-tuple-element.6), kind=kOutput, calls=%fused_computation.2 | convolution fusion | flops 196864 | bytes 67072 | tf_op jit(solution)/shard_map/dot_general | solution.py:41
  3.5 0.6 %broadcast.9 = s32[]{:T(128)} broadcast(s32[]{:T(128)} %constant.66), dimensions={} | broadcast | bytes 8 | tf_op args[5]
  4.1 1.3 %reduce.3 = s32[8,16]{1,0:T(8,128)S(1)} reduce(s32[8,16,1]{1,2,0:T(1,128)} %param.23, s32[]{:T(128)} %broadcast.9), dimensions={2}, to_apply=%param.23.reduce_sub_computation.3 | reduce | bytes 1028 | tf_op args[5]
  5.5 0.1 reshape.21.owners
  5.5 0.8 %copy.19.w_in = bf16[128,20]{1,0:T(8,128)(2,1)S(1)} copy(bf16[128,20]{0,1:T(8,128)(2,1)} %param.26) | data formatting | bytes 10240 | tf_op args[8]
  6.4 0.0 copy-start.7
  6.4 0.0 copy-start.8
  6.4 0.0 copy-start.9
  6.4 0.0 copy-start.10
  6.4 0.0 copy-start.11
  6.4 8.1 %shard_map.172.cond = bf16[16,64,128]{2,1,0:T(8,128)(2,1)} custom-call(bf16[4,64,128]{2,1,0:T(8,128)(2,1)} %part_ref.1), custom_call_target="tpu_custom_call" | custom-call | tf_op jit(solution)/shard_map/pallas_call | solution.py:84
  14.5 0.0 copy-done.2
  14.5 0.0 copy-done.7
  14.5 0.0 copy-done.8
  14.6 0.0 copy-done.9
  14.6 0.0 copy-done.10
  14.6 0.0 copy-done.11
  14.6 0.0 copy-start.1
  14.6 0.9 %copy-done.1 = bf16[16,64,128]{2,1,0:T(8,128)(2,1)S(1)} copy-done((bf16[16,64,128]{2,1,0:T(8,128)(2,1)S(1)}, bf16[16,64,128]{2,1,0:T(8,128)(2,1)}, u32[]{:S(2)}) %copy-start.1) | copy-done | bytes 262168
  15.5 0.0 copy-start.3
  15.5 1.0 %copy-done.3 = bf16[9,128,128]{2,1,0:T(8,128)(2,1)S(1)} copy-done((bf16[9,128,128]{2,1,0:T(8,128)(2,1)S(1)}, bf16[9,128,128]{2,1,0:T(8,128)(2,1)}, u32[]{:S(2)}) %copy-start.3) | copy-done | bytes 294936
  16.5 0.9 %copy-done.4 = f32[1,4,64,128]{3,2,1,0:T(8,128)S(1)} copy-done((f32[1,4,64,128]{3,2,1,0:T(8,128)S(1)}, f32[1,4,64,128]{3,2,1,0:T(8,128)}, u32[]{:S(2)}) %copy-start.4) | copy-done | bytes 131096
  17.4 0.9 %copy-done.5 = f32[1,4,64,128]{3,2,1,0:T(8,128)S(1)} copy-done((f32[1,4,64,128]{3,2,1,0:T(8,128)S(1)}, f32[1,4,64,128]{3,2,1,0:T(8,128)}, u32[]{:S(2)}) %copy-start.5) | copy-done | bytes 131096
  18.3 0.8 %copy-done.6 = s32[64,128]{1,0:T(8,128)S(1)} copy-done((s32[64,128]{1,0:T(8,128)S(1)}, s32[64,128]{1,0:T(8,128)}, u32[]{:S(2)}) %copy-start.6) | copy-done | bytes 32792
  19.1 28.1 %shard_map.173 = f32[4,64,128]{2,1,0:T(8,128)} custom-call(f32[8]{0:T(128)S(1)} %stack.23.scalars, s32[128]{0:T(128)S(1)} %reshape.21.owners, s32[128]{0:T(128)S(1)} %reshape.22.patch_rows, s32[128]{0:T(128)S(1)} %reshape.23.patch_cols, f32[4]{0:T(128)S(1)} %copy-done.9, bf16[16,64,128]{2,1,0:T(8,128)(2,1)S(1)} %copy-done.1, f32[4,64,128]{2,1,0:T(8,128)S(1)} %bitcast.25, ...), custom_call_target="tpu_custom_call" | custom-call | tf_op jit(solution)/shard_map/pallas_call | solution.py:343
  (4 shorter events, 0.0 us)
Async XLA Ops:
  0.0 2.7 %copy-start = (f32[128,128]{1,0:T(8,128)S(1)}, f32[128,128]{1,0:T(8,128)}, u32[]{:S(2)}) copy-start(f32[128,128]{1,0:T(8,128)} %param.28) | copy-start | bytes 196612
  0.0 14.5 %copy-start.2 = (f32[32,32,128]{2,1,0:T(8,128)S(1)}, f32[32,32,128]{2,1,0:T(8,128)}, u32[]{:S(2)}) copy-start(f32[32,32,128]{2,1,0:T(8,128)} %constant.47.clone.blend_cells) | copy-start | bytes 1572868
  6.4 8.2 %copy-start.7 = (f32[32,128]{1,0:T(8,128)S(1)}, f32[32,128]{1,0:T(8,128)}, u32[]{:S(2)}) copy-start(f32[32,128]{1,0:T(8,128)} %constant.48.clone.blend_lanes) | copy-start | bytes 49156
  6.4 8.2 %copy-start.8 = (bf16[4,128]{1,0:T(4,128)(2,1)S(1)}, bf16[4,128]{1,0:T(4,128)(2,1)}, u32[]{:S(2)}) copy-start(bf16[4,128]{1,0:T(4,128)(2,1)} %w_out.1) | copy-start | bytes 3076
  6.4 8.2 %copy-start.9 = (f32[4]{0:T(128)S(1)}, f32[4]{0:T(128)}, u32[]{:S(2)}) copy-start(f32[4]{0:T(128)} %b_out.1) | copy-start | bytes 52
  6.4 8.2 %copy-start.10 = (f32[128]{0:T(128)S(1)}, f32[128]{0:T(128)}, u32[]{:S(2)}) copy-start(f32[128]{0:T(128)} %param.30) | copy-start | bytes 1540
  6.4 8.2 %copy-start.11 = (f32[128]{0:T(128)S(1)}, f32[128]{0:T(128)}, u32[]{:S(2)}) copy-start(f32[128]{0:T(128)} %param.31) | copy-start | bytes 1540
  14.6 1.0 %copy-start.1 = (bf16[16,64,128]{2,1,0:T(8,128)(2,1)S(1)}, bf16[16,64,128]{2,1,0:T(8,128)(2,1)}, u32[]{:S(2)}) copy-start(bf16[16,64,128]{2,1,0:T(8,128)(2,1)} %shard_map.172.cond) | copy-start | bytes 786436
  15.5 1.0 %copy-start.3 = (bf16[9,128,128]{2,1,0:T(8,128)(2,1)S(1)}, bf16[9,128,128]{2,1,0:T(8,128)(2,1)}, u32[]{:S(2)}) copy-start(bf16[9,128,128]{2,1,0:T(8,128)(2,1)} %w_conv.1) | copy-start | bytes 884740
  16.5 0.9 %copy-start.4 = (f32[1,4,64,128]{3,2,1,0:T(8,128)S(1)}, f32[1,4,64,128]{3,2,1,0:T(8,128)}, u32[]{:S(2)}) copy-start(f32[1,4,64,128]{3,2,1,0:T(8,128)} %param.18) | copy-start | bytes 393220
  17.4 0.9 %copy-start.5 = (f32[1,4,64,128]{3,2,1,0:T(8,128)S(1)}, f32[1,4,64,128]{3,2,1,0:T(8,128)}, u32[]{:S(2)}) copy-start(f32[1,4,64,128]{3,2,1,0:T(8,128)} %param.19) | copy-start | bytes 393220
  18.3 0.8 %copy-start.6 = (s32[64,128]{1,0:T(8,128)S(1)}, s32[64,128]{1,0:T(8,128)}, u32[]{:S(2)}) copy-start(s32[64,128]{1,0:T(8,128)} %land.1) | copy-start | bytes 98308

commit v2 on v1

--- a/solution.py
+++ b/solution.py
@@ -17,29 +17,30 @@
 GAMMA = 0.25
 
 
-def sigma_at(index_value):
+def noise_plan(half_width):
+    index = np.arange(NSTEPS, dtype=np.float64)
     top_root = 800.0 ** (1.0 / 7.0)
     low_root = 0.002 ** (1.0 / 7.0)
-    fraction = index_value.astype(jnp.float32) / (NSTEPS - 1)
-    return (top_root + fraction * (low_root - top_root)) ** 7
-
-
-def precondition(step_index, w_emb):
-    sigma_now = sigma_at(step_index[0])
-    sigma_next = sigma_at(step_index[0] + 1)
+
+    def sigma_at(position):
+        return (top_root + position / (NSTEPS - 1) * (low_root - top_root)) ** 7
+
+    sigma_now = sigma_at(index)
+    sigma_next = sigma_at(index + 1)
     sigma_hat = (1.0 + GAMMA) * sigma_now
     sigma_sq_sum = sigma_hat * sigma_hat + SIGMA_DATA * SIGMA_DATA
-    scale_in = 1.0 / jnp.sqrt(sigma_sq_sum)
-    scale_skip = SIGMA_DATA * SIGMA_DATA / sigma_sq_sum
-    scale_out = SIGMA_DATA * sigma_hat / jnp.sqrt(sigma_sq_sum)
-    churn_scale = jnp.sqrt(GAMMA * (2.0 + GAMMA)) * sigma_now
-    noise_level = jnp.log(sigma_hat) / 4.0
-    half_width = w_emb.shape[1] // 2
-    frequency = jnp.exp(-jnp.log(10000.0) * jnp.arange(half_width, dtype=jnp.float32) / half_width)
-    angles = 1000.0 * noise_level * frequency
-    features = jnp.concatenate([jnp.cos(angles), jnp.sin(angles)])
-    embedding = jnp.dot(w_emb, features, precision=lax.Precision.HIGHEST)
-    return (sigma_hat, sigma_next, scale_in, scale_skip, scale_out, churn_scale, embedding)
+    columns = [
+        1.0 / np.sqrt(sigma_sq_sum),
+        np.sqrt(GAMMA * (2.0 + GAMMA)) * sigma_now,
+        SIGMA_DATA * SIGMA_DATA / sigma_sq_sum,
+        SIGMA_DATA * sigma_hat / np.sqrt(sigma_sq_sum),
+        (sigma_next - sigma_hat) / sigma_hat,
+    ]
+    columns += [np.zeros_like(index)] * (8 - len(columns))
+    frequency = np.exp(-np.log(10000.0) * np.arange(half_width) / half_width)
+    angles = 250.0 * np.log(sigma_hat)[:, None] * frequency[None, :]
+    features = np.concatenate([np.cos(angles), np.sin(angles)], axis=1)
+    return np.stack(columns, axis=1).reshape(-1).astype(np.float32), features.astype(np.float32)
 
 
 def window_weights(length):
@@ -84,8 +85,8 @@
     return pl.pallas_call(
         functools.partial(gather_kernel, axis_size),
         out_shape=jax.ShapeDtypeStruct(shape, part.dtype),
-        in_specs=[pl.BlockSpec(memory_space=pltpu.VMEM)],
-        out_specs=pl.BlockSpec(memory_space=pltpu.VMEM),
+        in_specs=[pl.BlockSpec(memory_space=pltpu.HBM)],
+        out_specs=pl.BlockSpec(memory_space=pltpu.HBM),
         scratch_shapes=[
             pltpu.SemaphoreType.DMA((axis_size - 1,)),
             pltpu.SemaphoreType.DMA((axis_size - 1,)),
@@ -116,24 +117,47 @@
 
 
 def tile_kernel(
-    scalars,
+    step_index,
+    plan_hbm,
+    owners_hbm,
+    patch_rows_hbm,
+    patch_cols_hbm,
+    b_out_hbm,
+    w_conv_hbm,
+    w_emb_hbm,
+    features_hbm,
+    b_in_hbm,
+    noisy_hbm,
+    churn_hbm,
+    cond_hbm,
+    w_in_hbm,
+    land_hbm,
+    gn_gain_hbm,
+    gn_bias_hbm,
+    blend_lanes_hbm,
+    blend_cells_hbm,
+    w_out_hbm,
+    out,
+    plan,
     owners,
     patch_rows,
     patch_cols,
     b_out,
-    cond,
+    w_conv,
+    w_emb,
+    features,
+    b_in,
     noisy,
     churn,
+    cond,
+    w_in,
     land,
-    bias_in,
-    w_in,
-    w_conv,
     gn_gain,
     gn_bias,
+    blend_lanes,
+    blend_cells,
     w_out,
-    blend_cells,
-    blend_lanes,
-    out,
+    operand_sem,
     row_list,
     col_list,
     inputs,
@@ -146,53 +170,45 @@
     weights,
     flat,
 ):
+    pairs = (
+        (plan_hbm, plan),
+        (owners_hbm, owners),
+        (patch_rows_hbm, patch_rows),
+        (patch_cols_hbm, patch_cols),
+        (b_out_hbm, b_out),
+        (w_conv_hbm, w_conv),
+        (w_emb_hbm, w_emb),
+        (features_hbm, features),
+        (b_in_hbm, b_in),
+        (noisy_hbm, noisy),
+        (churn_hbm, churn),
+        (cond_hbm, cond),
+        (w_in_hbm, w_in),
+        (land_hbm, land),
+        (gn_gain_hbm, gn_gain),
+        (gn_bias_hbm, gn_bias),
+        (blend_lanes_hbm, blend_lanes),
+        (blend_cells_hbm, blend_cells),
+        (w_out_hbm, w_out),
+    )
+    copies = [
+        pltpu.make_async_copy(source, target, operand_sem.at[index])
+        for index, (source, target) in enumerate(pairs)
+    ]
+    for copy in copies:
+        copy.start()
     self_tile = lax.axis_index("tile")
     channels = w_conv.shape[1]
     variables, tile_rows, tile_cols = noisy.shape
     cond_channels = cond.shape[0]
-    scale_in = scalars[0]
-    churn_scale = scalars[1]
-    scale_skip = scalars[2]
-    scale_out = scalars[3]
-    step_ratio = scalars[4]
-
-    def note_patch(index, count):
-        row_list[count] = patch_rows[index]
-        col_list[count] = patch_cols[index]
-        return count + (owners[index] == self_tile).astype(jnp.int32)
-
-    count = lax.fori_loop(0, owners.shape[0], note_patch, jnp.int32(0), unroll=8)
-
-    for channel in range(cond_channels):
-        inputs[channel * tile_rows : (channel + 1) * tile_rows, :] = cond[channel].astype(
-            jnp.float32
-        )
-    for variable in range(variables):
-        start = (cond_channels + variable) * tile_rows
-        x_hat = noisy[variable] + churn_scale * churn[variable]
-        inputs[start : start + tile_rows, :] = (
-            (scale_in * x_hat).astype(jnp.bfloat16).astype(jnp.float32)
-        )
-    used = cond_channels + variables
-    inputs[used * tile_rows :, :] = jnp.zeros(
-        ((K_IN - used) * tile_rows, tile_cols), jnp.float32
-    )
-    w_square[...] = jnp.zeros_like(w_square)
-    w_square[:, 0:used] = w_in[...].astype(jnp.float32)
-    w_first = w_square[...].T[0:K_IN].astype(jnp.bfloat16)
-    bias = bias_in[...]
-
-    def hidden_row(row, carry):
-        cells = inputs[pl.ds(row, K_IN, stride=tile_rows), :].T.astype(jnp.bfloat16)
-        pre_act = jnp.dot(cells, w_first, preferred_element_type=jnp.float32) + bias
-        hidden[row, LEAD : LEAD + tile_cols, :] = (
-            silu(pre_act).astype(jnp.bfloat16).astype(jnp.float32)
-        )
+
+    def clear_row(row, carry):
         total[row] = jnp.zeros((tile_cols, channels), jnp.float32)
         return carry
 
-    lax.fori_loop(0, tile_rows, hidden_row, 0, unroll=4)
-
+    lax.fori_loop(0, tile_rows, clear_row, 0, unroll=4)
+    for copy in copies:
+        copy.wait()
     zero_block = jnp.zeros((channels, channels), jnp.bfloat16)
     for col in range(3):
         tap = [w_conv[3 * a + col].astype(jnp.float32).T.astype(jnp.bfloat16) for a in range(3)]
@@ -211,6 +227,59 @@
         taps[col, 0, :, 0:channels] = jnp.zeros((PW, channels), jnp.bfloat16)
         taps[col, PH // 2, :, channels : 2 * channels] = jnp.zeros((PW, channels), jnp.bfloat16)
     weights[...] = jnp.zeros_like(weights)
+    step = step_index[0]
+    scale_in = plan[8 * step]
+    churn_scale = plan[8 * step + 1]
+    scale_skip = plan[8 * step + 2]
+    scale_out = plan[8 * step + 3]
+    step_ratio = plan[8 * step + 4]
+    feature = jnp.broadcast_to(features[pl.ds(step, 1), :], (8, features.shape[1]))
+    embedding = lax.dot_general(
+        feature,
+        w_emb[...],
+        (((1,), (1,)), ((), ())),
+        precision=lax.Precision.HIGHEST,
+        preferred_element_type=jnp.float32,
+    )
+    bias = b_in[...] + embedding[0:1]
+    slots = patch_rows.shape[1]
+
+    def note_patch(index, count):
+        for slot in range(slots):
+            row_list[count] = patch_rows[index, slot]
+            col_list[count] = patch_cols[index, slot]
+            count = count + (owners[index, 0, slot] == self_tile).astype(jnp.int32)
+        return count
+
+    count = lax.fori_loop(0, patch_rows.shape[0], note_patch, jnp.int32(0))
+
+    for channel in range(cond_channels):
+        inputs[channel * tile_rows : (channel + 1) * tile_rows, :] = cond[channel].astype(
+            jnp.float32
+        )
+    for variable in range(variables):
+        start = (cond_channels + variable) * tile_rows
+        x_hat = noisy[variable] + churn_scale * churn[variable]
+        inputs[start : start + tile_rows, :] = (
+            (scale_in * x_hat).astype(jnp.bfloat16).astype(jnp.float32)
+        )
+    used = cond_channels + variables
+    inputs[used * tile_rows :, :] = jnp.zeros(
+        ((K_IN - used) * tile_rows, tile_cols), jnp.float32
+    )
+    w_square[...] = jnp.zeros_like(w_square)
+    w_square[0:used, :] = w_in[...].astype(jnp.float32)
+    w_first = w_square[0:K_IN].astype(jnp.bfloat16)
+
+    def hidden_row(row, carry):
+        cells = inputs[pl.ds(row, K_IN, stride=tile_rows), :].T.astype(jnp.bfloat16)
+        pre_act = jnp.dot(cells, w_first, preferred_element_type=jnp.float32) + bias
+        hidden[row, LEAD : LEAD + tile_cols, :] = (
+            silu(pre_act).astype(jnp.bfloat16).astype(jnp.float32)
+        )
+        return carry
+
+    lax.fori_loop(0, tile_rows, hidden_row, 0, unroll=4)
 
     gain = jnp.concatenate([gn_gain[...], gn_gain[...]], axis=1)
     shift = jnp.concatenate([gn_bias[...], gn_bias[...]], axis=1)
@@ -318,14 +387,6 @@
     w_out,
     b_out,
 ):
-    sigma_hat, sigma_next, scale_in, scale_skip, scale_out, churn_scale, embedding = precondition(
-        step_index, w_emb
-    )
-    step_ratio = (sigma_next - sigma_hat) / sigma_hat
-    zero = jnp.zeros_like(scale_in)
-    scalars = jnp.stack(
-        [scale_in, churn_scale, scale_skip, scale_out, step_ratio, zero, zero, zero]
-    )
     cond = gather_members(coarse_cond, lax.axis_size("member"))
     channels = w_conv.shape[1]
     variables, tile_rows, tile_cols = noisy_state.shape[1:]
@@ -337,15 +398,40 @@
     blend_lanes = jnp.asarray(
         np.pad(blend, ((0, 0), (0, tile_cols - PW))).astype(np.float32)
     )
-    smem = pl.BlockSpec(memory_space=pltpu.SMEM)
-    vmem = pl.BlockSpec(memory_space=pltpu.VMEM)
+    plan, features = noise_plan(w_emb.shape[1] // 2)
+    operands = (
+        step_index,
+        jnp.asarray(plan),
+        jnp.transpose(owners, (0, 2, 1)),
+        patch_rows,
+        patch_cols,
+        b_out,
+        w_conv,
+        w_emb,
+        jnp.asarray(features),
+        b_in[None, :],
+        noisy_state[0],
+        churn_noise[0],
+        cond,
+        w_in.T,
+        land_mask,
+        gn_gain[None, :],
+        gn_bias[None, :],
+        blend_lanes,
+        blend_cells,
+        w_out,
+    )
     f32 = jnp.float32
     result = pl.pallas_call(
         tile_kernel,
         out_shape=jax.ShapeDtypeStruct((variables, tile_rows, tile_cols), f32),
-        in_specs=[smem] * 5 + [vmem] * 12,
-        out_specs=vmem,
-        scratch_shapes=[
+        in_specs=[pl.BlockSpec(memory_space=pltpu.SMEM)]
+        + [pl.BlockSpec(memory_space=pltpu.HBM)] * (len(operands) - 1),
+        out_specs=pl.BlockSpec(memory_space=pltpu.VMEM),
+        scratch_shapes=[pltpu.SMEM(value.shape, value.dtype) for value in operands[1:6]]
+        + [pltpu.VMEM(value.shape, value.dtype) for value in operands[6:]]
+        + [
+            pltpu.SemaphoreType.DMA((len(operands) - 1,)),
             pltpu.SMEM((slots + 1,), jnp.int32),
             pltpu.SMEM((slots + 1,), jnp.int32),
             pltpu.VMEM((K_IN * tile_rows, tile_cols), f32),
@@ -358,26 +444,8 @@
             pltpu.VMEM((tile_rows, tile_cols), f32),
             pltpu.VMEM((8 * tile_rows, tile_cols), f32),
         ],
-        compiler_params=pltpu.CompilerParams(vmem_limit_bytes=40 * 1024 * 1024),
-    )(
-        scalars,
-        owners.reshape(-1),
-        patch_rows.reshape(-1),
-        patch_cols.reshape(-1),
-        b_out,
-        cond,
-        noisy_state[0],
-        churn_noise[0],
-        land_mask,
-        (b_in + embedding)[None, :],
-        w_in,
-        w_conv,
-        gn_gain[None, :],
-        gn_bias[None, :],
-        w_out,
-        blend_cells,
-        blend_lanes,
-    )
+        compiler_params=pltpu.CompilerParams(vmem_limit_bytes=67108864),
+    )(*operands)
     return result[None]
 
 

time: 47.6 us -> 36.5 us (0.77)
  local copies, waits for them, and re-layouts: 7.58 us -> 0 us
  other arithmetic: 1.4 us -> 0 us
  matrix products: 0.87 us -> 0 us
  Pallas kernels: 36.2 us -> 35.7 us
    unnamed x26 -> x0, local copies, waits for them, and re-layouts: 5.88 us -> none
    reshape x3 -> x0, local copies, waits for them, and re-layouts: 1.61 us -> none  [the longest x1 0.77 us: body(): patch_cols.reshape(-1)]
    unnamed x1 -> x0, other arithmetic: 1.35 us -> none
    pallas_call x1, Pallas kernels: 8.11 us -> 6.89 us  [gather_members(): pl.pallas_call(functools.partial(gather_kernel, axis_size), out_shape=jax...]
    dot_general x1 -> x0, matrix products: 0.87 us -> none  [precondition(): embedding = jnp.dot(w_emb, features, precision=lax.Precision.HIGHEST)]
    pallas_call x1, Pallas kernels: 28.1 us -> 28.8 us  [body(): pl.pallas_call(tile_kernel, out_shape=jax.ShapeDtypeStruct((variables, ti...]
where the time goes in v2:
time: 36.5 us; the launch traced here: 36.4 us
  Pallas kernels  35.7 us (98%)
  between operations  0.66 us (2%)
    pallas_call x1, Pallas kernels, body(): pl.pallas_call(tile_kernel, out_shape=jax.ShapeDtypeStruct((variables, ti...  28.8 us
    pallas_call x1, Pallas kernels, gather_members(): pl.pallas_call(functools.partial(gather_kernel, axis_size), out_shape=jax...  6.89 us

profile of v2, /device:TPU:1, one launch (start us, length us, event | category | flops | bytes accessed | tf_op | source)
XLA Modules:
  0.0 36.4 jit_solution(16913771433000493584)
XLA Ops:
  0.7 6.9 %shard_map.190.cond_hbm = bf16[16,64,128]{2,1,0:T(8,128)(2,1)} custom-call(bf16[4,64,128]{2,1,0:T(8,128)(2,1)} %part_ref.1), custom_call_target="tpu_custom_call" | custom-call | tf_op jit(solution)/shard_map/pallas_call | solution.py:85
  7.5 28.8 %shard_map.191 = f32[4,64,128]{2,1,0:T(8,128)} custom-call(s32[1]{0:T(128)S(6)} %copy.22.step_index, f32[144]{0:T(256)} %constant.10.clone.plan_hbm, s32[8,1,16]{2,1,0:T(1,128)} %bitcast.13, s32[8,16]{1,0:T(8,128)} %patch_rows_hbm.1, s32[8,16]{1,0:T(8,128)} %patch_cols_hbm.1, f32[4]{0:T(128)} %b_out_hbm.1, bf16[9,128,128]{2,1,0:T(8,128)(2,1)} %w_conv_hbm.1, ...), custom_call_target="tpu_custom_call" | custom-call | tf_op jit(solution)/shard_map/pallas_call | solution.py:425

commit v3 on v2

--- a/solution.py
+++ b/solution.py
@@ -164,9 +164,12 @@
     w_square,
     hidden,
     total,
-    taps,
+    taps_even,
+    taps_odd,
     w_pairs,
-    conv,
+    conv_even,
+    conv_odd,
+    sums,
     weights,
     flat,
 ):
@@ -188,7 +191,7 @@
         (gn_gain_hbm, gn_gain),
         (gn_bias_hbm, gn_bias),
         (blend_lanes_hbm, blend_lanes),
-        (blend_cells_hbm, blend_cells),
+        (blend_cells_hbm, blend_cells.at[1]),
         (w_out_hbm, w_out),
     )
     copies = [
@@ -207,8 +210,8 @@
         return carry
 
     lax.fori_loop(0, tile_rows, clear_row, 0, unroll=4)
-    for copy in copies:
-        copy.wait()
+    blend_cells[0] = jnp.zeros(blend_cells.shape[1:], jnp.float32)
+    copies[5].wait()
     zero_block = jnp.zeros((channels, channels), jnp.bfloat16)
     for col in range(3):
         tap = [w_conv[3 * a + col].astype(jnp.float32).T.astype(jnp.bfloat16) for a in range(3)]
@@ -224,9 +227,15 @@
                         start + k * channels : start + (k + 1) * channels,
                         o * channels : (o + 1) * channels,
                     ] = blocks[half][k][o]
-        taps[col, 0, :, 0:channels] = jnp.zeros((PW, channels), jnp.bfloat16)
-        taps[col, PH // 2, :, channels : 2 * channels] = jnp.zeros((PW, channels), jnp.bfloat16)
+        for taps in (taps_even, taps_odd):
+            taps[col, 0, :, 0:channels] = jnp.zeros((PW, channels), jnp.bfloat16)
+            taps[col, PH // 2, :, channels : 2 * channels] = jnp.zeros(
+                (PW, channels), jnp.bfloat16
+            )
     weights[...] = jnp.zeros_like(weights)
+    for index, copy in enumerate(copies[:13]):
+        if index != 5:
+            copy.wait()
     step = step_index[0]
     scale_in = plan[8 * step]
     churn_scale = plan[8 * step + 1]
@@ -243,15 +252,8 @@
     )
     bias = b_in[...] + embedding[0:1]
     slots = patch_rows.shape[1]
-
-    def note_patch(index, count):
-        for slot in range(slots):
-            row_list[count] = patch_rows[index, slot]
-            col_list[count] = patch_cols[index, slot]
-            count = count + (owners[index, 0, slot] == self_tile).astype(jnp.int32)
-        return count
-
-    count = lax.fori_loop(0, patch_rows.shape[0], note_patch, jnp.int32(0))
+    scanned = patch_rows.shape[0] * slots // tile_rows
+    assert scanned * tile_rows == patch_rows.shape[0] * slots
 
     for channel in range(cond_channels):
         inputs[channel * tile_rows : (channel + 1) * tile_rows, :] = cond[channel].astype(
@@ -271,15 +273,23 @@
     w_square[0:used, :] = w_in[...].astype(jnp.float32)
     w_first = w_square[0:K_IN].astype(jnp.bfloat16)
 
-    def hidden_row(row, carry):
+    def hidden_row(row, count):
         cells = inputs[pl.ds(row, K_IN, stride=tile_rows), :].T.astype(jnp.bfloat16)
         pre_act = jnp.dot(cells, w_first, preferred_element_type=jnp.float32) + bias
         hidden[row, LEAD : LEAD + tile_cols, :] = (
             silu(pre_act).astype(jnp.bfloat16).astype(jnp.float32)
         )
-        return carry
-
-    lax.fori_loop(0, tile_rows, hidden_row, 0, unroll=4)
+        for entry in range(scanned):
+            worker = (row * scanned + entry) // slots
+            slot = (row * scanned + entry) % slots
+            row_list[count] = patch_rows[worker, slot]
+            col_list[count] = patch_cols[worker, slot]
+            count = count + (owners[worker, 0, slot] == self_tile).astype(jnp.int32)
+        return count
+
+    count = lax.fori_loop(0, tile_rows, hidden_row, jnp.int32(0), unroll=8)
+    for copy in copies[13:]:
+        copy.wait()
 
     gain = jnp.concatenate([gn_gain[...], gn_gain[...]], axis=1)
     shift = jnp.concatenate([gn_bias[...], gn_bias[...]], axis=1)
@@ -292,10 +302,10 @@
         value = group_sum(value[:, 0:channels] + value[:, channels : 2 * channels])
         return jnp.concatenate([value, value], axis=1)
 
-    def one_patch(slot, carry):
+    def convolve(slot, taps, conv, parity):
+        slot = jnp.minimum(slot, jnp.maximum(count - 1, 0))
         row_start = row_list[slot]
         col_start = col_list[slot]
-        weights[pl.ds(row_start, PH), :] += pltpu.roll(lanes, col_start, 1)
         for i in range(PH):
             pair = (i + 1) // 2
             lane = 0 if i % 2 else channels
@@ -317,10 +327,24 @@
         )
         convolved = jnp.dot(left, w_pairs[...], preferred_element_type=jnp.float32)
         conv[...] = convolved
-        mean = spread(jnp.sum(convolved, axis=0, keepdims=True)) * inverse
-        centred = conv[...] - mean
-        var = spread(jnp.sum(centred * centred, axis=0, keepdims=True)) * inverse
+        sums[parity : parity + 1, :] = jnp.sum(convolved, axis=0, keepdims=True)
+
+    def finish(slot, conv, parity):
+        live = (slot < count).astype(jnp.int32)
+        slot = jnp.minimum(slot, count - 1)
+        row_start = row_list[slot]
+        col_start = col_list[slot]
+        mean = spread(sums[parity : parity + 1, :]) * inverse
+        squares = jnp.zeros((8, 2 * channels), jnp.float32)
+        for t in range(PH // 2):
+            centred = conv[t * PW : (t + 1) * PW, :] - mean
+            centred = (centred * centred).reshape(PW // 8, 8, 2 * channels)
+            squares = squares + jnp.sum(centred, axis=0)
+        var = spread(jnp.sum(squares, axis=0, keepdims=True)) * inverse
         scale = lax.rsqrt(var + 1e-06) * gain
+        weights[pl.ds(row_start, PH), :] += pltpu.roll(
+            lanes * live.astype(jnp.float32), col_start, 1
+        )
         for t in range(PH // 2):
             normed = (conv[t * PW : (t + 1) * PW, :] - mean) * scale + shift
             active = silu(normed)
@@ -332,10 +356,19 @@
                     .astype(jnp.bfloat16)
                     .astype(jnp.float32)
                 )
-                total[row_start + i, pl.ds(col_start, PW), :] += residual * blend_cells[i]
+                total[row_start + i, pl.ds(col_start, PW), :] += residual * blend_cells[live, i]
+
+    convolve(0, taps_even, conv_even, 0)
+
+    def two_patches(turn, carry):
+        slot = 2 * turn
+        convolve(slot + 1, taps_odd, conv_odd, 1)
+        finish(slot, conv_even, 0)
+        convolve(slot + 2, taps_even, conv_even, 0)
+        finish(slot + 1, conv_odd, 1)
         return carry
 
-    lax.fori_loop(0, count, one_patch, 0)
+    lax.fori_loop(0, (count + 1) // 2, two_patches, 0)
 
     w_square[0:16, :] = jnp.zeros((16, channels), jnp.float32)
     w_square[0:variables, :] = w_out[...].astype(jnp.float32)
@@ -429,7 +462,8 @@
         + [pl.BlockSpec(memory_space=pltpu.HBM)] * (len(operands) - 1),
         out_specs=pl.BlockSpec(memory_space=pltpu.VMEM),
         scratch_shapes=[pltpu.SMEM(value.shape, value.dtype) for value in operands[1:6]]
-        + [pltpu.VMEM(value.shape, value.dtype) for value in operands[6:]]
+        + [pltpu.VMEM(value.shape, value.dtype) for value in operands[6:-2]]
+        + [pltpu.VMEM((2,) + blend_cells.shape, f32), pltpu.VMEM(w_out.shape, w_out.dtype)]
         + [
             pltpu.SemaphoreType.DMA((len(operands) - 1,)),
             pltpu.SMEM((slots + 1,), jnp.int32),
@@ -439,8 +473,11 @@
             pltpu.VMEM((tile_rows, tile_cols + 2 * LEAD, channels), f32),
             pltpu.VMEM((tile_rows, tile_cols, channels), f32),
             pltpu.VMEM((3, PH // 2 + 1, PW, 2 * channels), jnp.bfloat16),
+            pltpu.VMEM((3, PH // 2 + 1, PW, 2 * channels), jnp.bfloat16),
             pltpu.VMEM((12 * channels, 2 * channels), jnp.bfloat16),
             pltpu.VMEM((PH * PW // 2, 2 * channels), f32),
+            pltpu.VMEM((PH * PW // 2, 2 * channels), f32),
+            pltpu.VMEM((2, 2 * channels), f32),
             pltpu.VMEM((tile_rows, tile_cols), f32),
             pltpu.VMEM((8 * tile_rows, tile_cols), f32),
         ],

time: 36.5 us -> 30.1 us (0.82)
  Pallas kernels: 35.7 us -> 29.3 us
    pallas_call x1, Pallas kernels: 28.8 us -> 22.4 us  [body(): pl.pallas_call(tile_kernel, out_shape=jax.ShapeDtypeStruct((variables, ti...]
where the time goes in v3:
time: 30.1 us; the launch traced here: 30 us
  Pallas kernels  29.3 us (97%)
  between operations  0.66 us (2%)
    pallas_call x1, Pallas kernels, body(): pl.pallas_call(tile_kernel, out_shape=jax.ShapeDtypeStruct((variables, ti...  22.4 us
    pallas_call x1, Pallas kernels, gather_members(): pl.pallas_call(functools.partial(gather_kernel, axis_size), out_shape=jax...  6.89 us

profile of v3, /device:TPU:1, one launch (start us, length us, event | category | flops | bytes accessed | tf_op | source)
XLA Modules:
  0.0 30.0 jit_solution(5354145290212021464)
XLA Ops:
  0.7 6.9 %shard_map.190.cond_hbm = bf16[16,64,128]{2,1,0:T(8,128)(2,1)} custom-call(bf16[4,64,128]{2,1,0:T(8,128)(2,1)} %part_ref.1), custom_call_target="tpu_custom_call" | custom-call | tf_op jit(solution)/shard_map/pallas_call | solution.py:85
  7.5 22.4 %shard_map.191 = f32[4,64,128]{2,1,0:T(8,128)} custom-call(s32[1]{0:T(128)S(6)} %copy.22.step_index, f32[144]{0:T(256)} %constant.10.clone.plan_hbm, s32[8,1,16]{2,1,0:T(1,128)} %bitcast.13, s32[8,16]{1,0:T(8,128)} %patch_rows_hbm.1, s32[8,16]{1,0:T(8,128)} %patch_cols_hbm.1, f32[4]{0:T(128)} %b_out_hbm.1, bf16[9,128,128]{2,1,0:T(8,128)(2,1)} %w_conv_hbm.1, ...), custom_call_target="tpu_custom_call" | custom-call | tf_op jit(solution)/shard_map/pallas_call | solution.py:458

commit v4 on v3

--- a/solution.py
+++ b/solution.py
@@ -296,7 +296,7 @@
     lanes = blend_lanes[...]
     cell_count = PH * PW
     inverse = 1.0 / (4 * cell_count)
-    position = lax.broadcasted_iota(jnp.int32, (PW, channels), 0)
+    position = lax.broadcasted_iota(jnp.int32, (8, channels), 0)
 
     def spread(value):
         value = group_sum(value[:, 0:channels] + value[:, channels : 2 * channels])
@@ -312,9 +312,11 @@
             for col in range(3):
                 piece = hidden[row_start + i, pl.ds(col_start + (LEAD - 1 + col), PW), :]
                 if col == 0:
-                    piece = jnp.where(position == 0, 0.0, piece)
+                    edge = jnp.where(position == 0, 0.0, piece[0:8])
+                    piece = jnp.concatenate([edge, piece[8:PW]], axis=0)
                 if col == 2:
-                    piece = jnp.where(position == PW - 1, 0.0, piece)
+                    edge = jnp.where(position == 7, 0.0, piece[PW - 8 : PW])
+                    piece = jnp.concatenate([piece[0 : PW - 8], edge], axis=0)
                 taps[col, pair, :, lane : lane + channels] = piece.astype(jnp.bfloat16)
         half_cells = cell_count // 2
         left = jnp.concatenate(
@@ -345,27 +347,27 @@
         weights[pl.ds(row_start, PH), :] += pltpu.roll(
             lanes * live.astype(jnp.float32), col_start, 1
         )
-        for t in range(PH // 2):
-            normed = (conv[t * PW : (t + 1) * PW, :] - mean) * scale + shift
-            active = silu(normed)
-            for o in range(2):
-                i = 2 * t + o
-                own = hidden[row_start + i, pl.ds(col_start + LEAD, PW), :]
-                residual = (
-                    (own + active[:, o * channels : (o + 1) * channels])
-                    .astype(jnp.bfloat16)
-                    .astype(jnp.float32)
-                )
-                total[row_start + i, pl.ds(col_start, PW), :] += residual * blend_cells[live, i]
+        for quad in range(PH // 4):
+            parts = []
+            for t in (2 * quad, 2 * quad + 1):
+                normed = (conv[t * PW : (t + 1) * PW, :] - mean) * scale + shift
+                active = silu(normed)
+                parts += [active[:, 0:channels], active[:, channels : 2 * channels]]
+            cells = pl.ds(row_start + 4 * quad, 4)
+            own = hidden[cells, pl.ds(col_start + LEAD, PW), :]
+            residual = (own + jnp.stack(parts)).astype(jnp.bfloat16).astype(jnp.float32)
+            total[cells, pl.ds(col_start, PW), :] += (
+                residual * blend_cells[live, 4 * quad : 4 * quad + 4]
+            )
 
     convolve(0, taps_even, conv_even, 0)
 
     def two_patches(turn, carry):
         slot = 2 * turn
+        finish(slot, conv_even, 0)
         convolve(slot + 1, taps_odd, conv_odd, 1)
-        finish(slot, conv_even, 0)
+        finish(slot + 1, conv_odd, 1)
         convolve(slot + 2, taps_even, conv_even, 0)
-        finish(slot + 1, conv_odd, 1)
         return carry
 
     lax.fori_loop(0, (count + 1) // 2, two_patches, 0)
@@ -391,7 +393,7 @@
             ]
         return carry
 
-    lax.fori_loop(0, tile_rows // 8, project, 0)
+    lax.fori_loop(0, tile_rows // 8, project, 0, unroll=2)
 
     cover = weights[...]
     land_value = land[...].astype(jnp.float32) / jnp.maximum(cover, 0.25)

time: 30.1 us -> 29.5 us (0.980)
  Pallas kernels: 29.3 us -> 28.7 us
    pallas_call x1, Pallas kernels: 22.4 us -> 21.8 us  [body(): pl.pallas_call(tile_kernel, out_shape=jax.ShapeDtypeStruct((variables, ti...]
where the time goes in v4:
time: 29.5 us; the launch traced here: 29.4 us
  Pallas kernels  28.7 us (97%)
  between operations  0.66 us (2%)
    pallas_call x1, Pallas kernels, body(): pl.pallas_call(tile_kernel, out_shape=jax.ShapeDtypeStruct((variables, ti...  21.8 us
    pallas_call x1, Pallas kernels, gather_members(): pl.pallas_call(functools.partial(gather_kernel, axis_size), out_shape=jax...  6.89 us

profile of v4, /device:TPU:1, one launch (start us, length us, event | category | flops | bytes accessed | tf_op | source)
XLA Modules:
  0.0 29.4 jit_solution(2754077248990100096)
XLA Ops:
  0.7 6.9 %shard_map.190.cond_hbm = bf16[16,64,128]{2,1,0:T(8,128)(2,1)} custom-call(bf16[4,64,128]{2,1,0:T(8,128)(2,1)} %part_ref.1), custom_call_target="tpu_custom_call" | custom-call | tf_op jit(solution)/shard_map/pallas_call | solution.py:85
  7.5 21.8 %shard_map.191 = f32[4,64,128]{2,1,0:T(8,128)} custom-call(s32[1]{0:T(128)S(6)} %copy.22.step_index, f32[144]{0:T(256)} %constant.10.clone.plan_hbm, s32[8,1,16]{2,1,0:T(1,128)} %bitcast.13, s32[8,16]{1,0:T(8,128)} %patch_rows_hbm.1, s32[8,16]{1,0:T(8,128)} %patch_cols_hbm.1, f32[4]{0:T(128)} %b_out_hbm.1, bf16[9,128,128]{2,1,0:T(8,128)(2,1)} %w_conv_hbm.1, ...), custom_call_target="tpu_custom_call" | custom-call | tf_op jit(solution)/shard_map/pallas_call | solution.py:460
